TPU v7x, 256 devices: a whole 4x4x8 slice. The times are simulated.
256 devices in a mesh: row: 32 (over z, x), col: 8 (over y, core).
Axes of the slice: x: 4, y: 4, z: 8, core: 2. Of those that a mesh axis runs over, the one named last changes fastest.
Arguments:
- image: bfloat16 [512, 1024, 256], P('row', 'col'), may hold values from -6 to 6
- kernel_one: bfloat16 [3, 3, 256, 256], replicated, may hold values from -0.125 to 0.125
- kernel_two: bfloat16 [3, 3, 256, 512], replicated, may hold values from -0.125 to 0.125
- cotangent: bfloat16 [256, 512, 512], P('row', 'col'), may hold values from -6 to 6
Outputs:
- image_grad: bfloat16 [512, 1024, 256], P('row', 'col')
- update_one: bfloat16 [3, 3, 256, 256], replicated
- update_two: bfloat16 [3, 3, 256, 512], replicated
All inputs are finite; a program needn't handle non-finite values.
Results may differ from a plain program's by a relative error of at most 0.006.
Values may be sent and summed in bfloat16 or wider, within the bound.
A program may use at most 128 MiB of HBM per device.

v0:
```python
import jax
import jax.numpy as jnp
from jax import lax
from jax.sharding import PartitionSpec as P


def padded(shard, sides, width):
    for axis, dim in sides:
        size, length = (lax.axis_size(axis), shard.shape[dim])
        up = [(i, (i + 1) % size) for i in range(size - 1)]
        down = [(j, i) for i, j in up]
        last = lax.slice_in_dim(shard, length - width, length, axis=dim)
        initial = lax.slice_in_dim(shard, 0, width, axis=dim)
        before = lax.ppermute(last, axis, up)
        after = lax.ppermute(initial, axis, down)
        shard = jnp.concatenate([before, shard, after], axis=dim)
    return shard


def passed_along(shard, axis, by):
    size = lax.axis_size(axis)
    pairs = [(i, i + by) for i in range(size) if 0 <= i + by < size]
    return lax.ppermute(shard, axis, pairs)


def conv_local(source, kernel, padding, dilation, layout):
    result = lax.conv_general_dilated(
        source[None],
        kernel,
        (1, 1),
        padding,
        lhs_dilation=dilation,
        dimension_numbers=("NHWC", layout, "NHWC"),
        preferred_element_type=jnp.float32,
    )
    return result[0]


def on_device(image, kernel_one, kernel_two, cotangent):
    rows_here = image.shape[0]
    cols_here = image.shape[1]
    image_pad = padded(image, (("row", 0), ("col", 1)), 1)
    pre_act = conv_local(image_pad, kernel_one, "VALID", (1, 1), "HWIO")
    activ = jax.nn.silu(pre_act).astype(jnp.bfloat16)
    left_edge = passed_along(activ[:, -1:], "col", 1)
    act_cols = jnp.concatenate([left_edge, activ], 1)
    top_edge = passed_along(act_cols[-1:], "row", 1)
    act_pad = jnp.concatenate([top_edge, act_cols], 0)
    rows_two = []
    for row_off in range(3):
        cols_two = []
        for col_off in range(3):
            patch = act_pad[
                row_off : row_off + rows_here - 1 : 2, col_off : col_off + cols_here - 1 : 2
            ]
            cols_two.append(
                jnp.einsum("ijc,ije->ce", patch, cotangent, preferred_element_type=jnp.float32)
            )
        rows_two.append(jnp.stack(cols_two))
    grad_two = jnp.stack(rows_two)
    flipped_two = kernel_two[::-1, ::-1]
    act_full = conv_local(cotangent, flipped_two, ((2, 2), (2, 2)), (2, 2), "HWOI")
    from_right = passed_along(act_full[:, :1], "col", -1)
    act_trim = act_full[:, 1:]
    act_trim = jnp.concatenate([act_trim[:, :-1], act_trim[:, -1:] + from_right], 1)
    from_below = passed_along(act_trim[:1].astype(jnp.bfloat16), "row", -1).astype(jnp.float32)
    act_grad = act_trim[1:]
    act_grad = jnp.concatenate([act_grad[:-1], act_grad[-1:] + from_below], 0)
    sig = jax.nn.sigmoid(pre_act)
    pre_grad = (act_grad * sig * (1.0 + pre_act * (1.0 - sig))).astype(jnp.bfloat16)
    rows_one = []
    for row_off in range(3):
        cols_one = []
        for col_off in range(3):
            patch = image_pad[row_off : row_off + rows_here, col_off : col_off + cols_here]
            cols_one.append(
                jnp.einsum("ijc,ijd->cd", patch, pre_grad, preferred_element_type=jnp.float32)
            )
        rows_one.append(jnp.stack(cols_one))
    grad_one = jnp.stack(rows_one)
    grad_pad = padded(pre_grad, (("row", 0), ("col", 1)), 1)
    image_grad = conv_local(grad_pad, kernel_one[::-1, ::-1], "VALID", (1, 1), "HWOI").astype(
        jnp.bfloat16
    )
    flat_one = grad_one.reshape(-1)
    flat_two = grad_two.reshape(-1)
    total_one, total_two = lax.psum((flat_one, flat_two), ("row", "col"))
    update_one = (total_one * lax.rsqrt(jnp.mean(total_one * total_one) + 1e-06)).astype(
        jnp.bfloat16
    )
    update_two = (total_two * lax.rsqrt(jnp.mean(total_two * total_two) + 1e-06)).astype(
        jnp.bfloat16
    )
    return (image_grad, update_one.reshape(kernel_one.shape), update_two.reshape(kernel_two.shape))


def solution(mesh):
    placed = (P("row", "col", None), P(), P(), P("row", "col", None))
    return jax.shard_map(
        on_device,
        mesh=mesh,
        in_specs=placed,
        out_specs=(P("row", "col", None), P(), P()),
        check_vma=False,
    )
```

profile of v0, /device:TPU:2, one launch (start us, length us, event | category | flops | bytes accessed | tf_op | source)
XLA Modules:
  0.0 440.2 jit_solution(7343728317577428346)
XLA Ops:
  10.7 2.6 copy.37
  13.3 4.1 reshape.29
  22.8 3.4 collective-permute-start.2
  26.2 2.4 collective-permute-start.3
  36.8 2.5 collective-permute-start.4
  47.9 4.4 maximum_bitcast_fusion
  52.3 3.9 copy.64
  56.2 2.5 pad.2.clone
  58.6 3.2 reshape.32
  63.8 3.0 convolution_select_fusion.1
  66.9 3.6 maximum_maximum_fusion
  74.7 2.7 slice.143
  77.4 2.7 slice.142
  80.1 2.7 slice.146
  82.8 2.7 slice.145
  91.0 4.4 %collective-permute-start.10 = (bf16[16,1,256]{2,1,0:T(2,128)(2,1)S(1)}, bf16[16,1,256]{2,1,0:T(2,128)(2,1)S(1)}, u32[]{:S(2)}, u32[]{:S(2)}) collective-permute-start(bf16[16,1,256]{2,1,0:T(2,128)(2,1)S(1)} %slice.178), channel_id=1, source_target_pairs={{0,1},{1,2},{2,3},{3,4},{4,5},{5,6},{6,7},{8,9},{9,10},{10,11},{11... | collective-permute-start | bytes 24584 | tf_op jit(solution)/shard_map/ppermute | solution.py:23
  101.3 2.6 copy.65
  104.3 2.7 slice.141
  107.5 3.8 collective-permute-start.11
  115.7 2.7 slice.140
  118.4 2.7 slice.139
  127.9 3.4 copy.66
  131.3 4.7 %collective-permute-start.6 = (bf16[1,128,256]{2,1,0:T(8,128)(2,1)S(1)}, bf16[1,128,256]{2,1,0:T(8,128)(2,1)S(1)}, u32[]{:S(2)}, u32[]{:S(2)}) collective-permute-start(bf16[1,128,256]{2,1,0:T(8,128)(2,1)S(1)} %get-tuple-element.19), channel_id=1, source_target_pairs={{0,8},{8,16},{16,24},{24,32},{32,40},{40,48},{48,56},{56,64},{64,7... | collective-permute-start | bytes 196616 | tf_op jit(solution)/shard_map/ppermute | solution.py:14
  138.0 5.9 %collective-permute-done.7 = bf16[1,128,256]{2,1,0:T(8,128)(2,1)S(1)} collective-permute-done((bf16[1,128,256]{2,1,0:T(8,128)(2,1)S(1)}, bf16[1,128,256]{2,1,0:T(8,128)(2,1)S(1)}, u32[]{:S(2)}, u32[]{:S(2)}) %collective-permute-start.7) | collective-permute-done | bytes 65568 | tf_op jit(solution)/shard_map/ppermute | solution.py:15
  143.9 2.5 collective-permute-start.8
  148.0 3.1 collective-permute-done.9
  156.7 2.8 select_convert_fusion
  161.1 255.9 %all-reduce.3.cloned.1.call-done = (f32[589824]{0:T(1024)}, f32[1179648]{0:T(1024)}) async-done(((f32[589824]{0:T(1024)}, f32[1179648]{0:T(1024)}), (f32[589824]{0:T(1024)}, f32[1179648]{0:T(1024)})) %all-reduce.3.cloned.1.call-update) | async-done | bytes 7077904 | tf_op jit(solution)/shard_map/psum | solution.py:87
  417.1 3.6 multiply_reduce_fusion
  421.3 2.5 multiply_convert_fusion
  423.9 2.7 reshape.22
  426.6 2.9 multiply_reduce_fusion.1
  (140 shorter events, 68.8 us)
Async XLA Ops:
  7.2 409.9 %all-reduce.3.cloned.1.call-start = ((), (), s32[]{:S(2)}) async-start(), calls=%async_computation | async-start | bytes 14155776 | tf_op jit(solution)/shard_map/psum | solution.py:87
  17.4 4.7 %copy-start.9 = (bf16[16,128,256]{2,1,0:T(8,128)(2,1)S(1)}, bf16[16,128,256]{2,1,0:T(8,128)(2,1)}, u32[]{:S(2)}) copy-start(bf16[16,128,256]{2,1,0:T(8,128)(2,1)} %param.4) | copy-start | bytes 3145732
  20.8 9.8 %collective-permute-start = (f32[17,1,256]{2,1,0:T(1,128)S(1)}, f32[17,1,256]{2,1,0:T(1,128)S(1)}, u32[]{:S(2)}, u32[]{:S(2)}) collective-permute-start(f32[17,1,256]{2,1,0:T(1,128)S(1)} %slice.157), channel_id=1, source_target_pairs={{1,0},{2,1},{3,2},{4,3},{5,4},{6,5},{7,6},{9,8},{10,9},{11,10},{12... | collective-permute-start | bytes 52232 | tf_op jit(solution)/shard_map/ppermute | solution.py:23
  22.8 10.2 %collective-permute-start.2 = (bf16[1,128,256]{1,2,0:T(8,128)(2,1)S(1)}, bf16[1,128,256]{1,2,0:T(8,128)(2,1)S(1)}, u32[]{:S(2)}, u32[]{:S(2)}) collective-permute-start(bf16[1,128,256]{1,2,0:T(8,128)(2,1)S(1)} %get-tuple-element.21), channel_id=1, source_target_pairs={{0,8},{8,16},{16,24},{24,32},{32,40},{40,48},{48,56},{56,64},{64,7... | collective-permute-start | bytes 196616 | tf_op jit(solution)/shard_map/ppermute | solution.py:14
  26.2 6.8 %collective-permute-start.3 = (bf16[1,128,256]{1,2,0:T(8,128)(2,1)S(1)}, bf16[1,128,256]{1,2,0:T(8,128)(2,1)S(1)}, u32[]{:S(2)}, u32[]{:S(2)}) collective-permute-start(bf16[1,128,256]{1,2,0:T(8,128)(2,1)S(1)} %get-tuple-element.22), channel_id=1, source_target_pairs={{8,0},{16,8},{24,16},{32,24},{40,32},{48,40},{56,48},{64,56},{72,6... | collective-permute-start | bytes 196616 | tf_op jit(solution)/shard_map/ppermute | solution.py:15
  36.8 8.1 %collective-permute-start.4 = (bf16[18,1,256]{2,0,1:T(8,128)(2,1)S(1)}, bf16[18,1,256]{2,0,1:T(8,128)(2,1)S(1)}, u32[]{:S(2)}, u32[]{:S(2)}) collective-permute-start(bf16[18,1,256]{2,0,1:T(8,128)(2,1)S(1)} %copy.41), channel_id=1, source_target_pairs={{0,1},{1,2},{2,3},{3,4},{4,5},{5,6},{6,7},{8,9},{9,10},{10,11},{11... | collective-permute-start | bytes 27656 | tf_op jit(solution)/shard_map/ppermute | solution.py:14
  41.1 5.4 %collective-permute-start.5 = (bf16[18,1,256]{2,0,1:T(8,128)(2,1)S(1)}, bf16[18,1,256]{2,0,1:T(8,128)(2,1)S(1)}, u32[]{:S(2)}, u32[]{:S(2)}) collective-permute-start(bf16[18,1,256]{2,0,1:T(8,128)(2,1)S(1)} %copy.42), channel_id=1, source_target_pairs={{1,0},{2,1},{3,2},{4,3},{5,4},{6,5},{7,6},{9,8},{10,9},{11,10},{12... | collective-permute-start | bytes 27656 | tf_op jit(solution)/shard_map/ppermute | solution.py:15
  43.1 28.3 %collective-permute-start.1 = (bf16[1,128,256]{2,1,0:T(8,128)(2,1)}, bf16[1,128,256]{2,1,0:T(8,128)(2,1)S(1)}, u32[]{:S(2)}, u32[]{:S(2)}) collective-permute-start(bf16[1,128,256]{2,1,0:T(8,128)(2,1)} %fusion.41), channel_id=1, source_target_pairs={{8,0},{16,8},{24,16},{32,24},{40,32},{48,40},{56,48},{64,56},{72,6... | collective-permute-start | bytes 196616 | tf_op jit(solution)/shard_map/ppermute | solution.py:23
  61.9 1.9 copy-start.26
  63.8 3.0 copy-start.2
  63.8 3.0 copy-start.3
  85.5 2.0 copy-start.8
  85.5 2.7 copy-start.7
  90.0 5.5 %copy-start.14 = (bf16[8,64,512]{2,1,0:T(8,128)(2,1)S(1)}, bf16[8,64,512]{2,1,0:T(8,128)(2,1)}, u32[]{:S(2)}) copy-start(bf16[8,64,512]{2,1,0:T(8,128)(2,1)} %param.7) | copy-start | bytes 1572868
  90.0 5.5 %copy-start.21 = (bf16[8,64,256]{2,1,0:T(8,128)(2,1)S(1)}, bf16[8,64,256]{2,1,0:T(8,128)(2,1)}, u32[]{:S(2)}) copy-start(bf16[8,64,256]{2,1,0:T(8,128)(2,1)} %slice.143) | copy-start | bytes 786436
  90.4 6.2 %copy-start.20 = (bf16[8,64,256]{2,1,0:T(8,128)(2,1)S(1)}, bf16[8,64,256]{2,1,0:T(8,128)(2,1)}, u32[]{:S(2)}) copy-start(bf16[8,64,256]{2,1,0:T(8,128)(2,1)} %slice.142) | copy-start | bytes 786436
  91.0 6.8 %copy-start.19 = (bf16[8,64,256]{2,1,0:T(8,128)(2,1)S(1)}, bf16[8,64,256]{2,1,0:T(8,128)(2,1)}, u32[]{:S(2)}) copy-start(bf16[8,64,256]{2,1,0:T(8,128)(2,1)} %slice.146) | copy-start | bytes 786436
  91.0 7.9 %copy-start.18 = (bf16[8,64,256]{2,1,0:T(8,128)(2,1)S(1)}, bf16[8,64,256]{2,1,0:T(8,128)(2,1)}, u32[]{:S(2)}) copy-start(bf16[8,64,256]{2,1,0:T(8,128)(2,1)} %slice.145) | copy-start | bytes 786436
  91.0 12.9 %collective-permute-start.10 = (bf16[16,1,256]{2,1,0:T(2,128)(2,1)S(1)}, bf16[16,1,256]{2,1,0:T(2,128)(2,1)S(1)}, u32[]{:S(2)}, u32[]{:S(2)}) collective-permute-start(bf16[16,1,256]{2,1,0:T(2,128)(2,1)S(1)} %slice.178), channel_id=1, source_target_pairs={{0,1},{1,2},{2,3},{3,4},{4,5},{5,6},{6,7},{8,9},{9,10},{10,11},{11... | collective-permute-start | bytes 24584 | tf_op jit(solution)/shard_map/ppermute | solution.py:23
  103.9 9.7 %copy-start.22 = (bf16[16,1,256]{2,1,0:T(2,128)(2,1)}, bf16[16,1,256]{2,1,0:T(2,128)(2,1)S(1)}, u32[]{:S(2)}) copy-start(bf16[16,1,256]{2,1,0:T(2,128)(2,1)S(1)} %collective-permute-done.10) | copy-start | bytes 24580
  107.5 6.1 %copy-start.15 = (bf16[8,64,512]{2,1,0:T(8,128)(2,1)S(1)}, bf16[8,64,512]{2,1,0:T(8,128)(2,1)}, u32[]{:S(2)}) copy-start(bf16[8,64,512]{2,1,0:T(8,128)(2,1)} %param.7) | copy-start | bytes 1572868
  107.5 6.4 %copy-start.16 = (f32[1,256,512]{2,1,0:T(8,128)S(1)}, f32[1,256,512]{2,1,0:T(8,128)}, u32[]{:S(2)}) copy-start(f32[1,256,512]{2,1,0:T(8,128)} %convolution_bitcast_fusion) | copy-start | bytes 1572868
  107.5 6.4 %copy-start.17 = (f32[1,256,512]{2,1,0:T(8,128)S(1)}, f32[1,256,512]{2,1,0:T(8,128)}, u32[]{:S(2)}) copy-start(f32[1,256,512]{2,1,0:T(8,128)} %convolution_bitcast_fusion.1) | copy-start | bytes 1572868
  107.5 7.7 %collective-permute-start.11 = (bf16[1,129,256]{2,1,0:T(8,128)(2,1)S(1)}, bf16[1,129,256]{2,1,0:T(8,128)(2,1)S(1)}, u32[]{:S(2)}, u32[]{:S(2)}) collective-permute-start(bf16[1,129,256]{2,1,0:T(8,128)(2,1)S(1)} %fusion.42), channel_id=1, source_target_pairs={{0,8},{8,16},{16,24},{24,32},{32,40},{40,48},{48,56},{56,64},{64,7... | collective-permute-start | bytes 198152 | tf_op jit(solution)/shard_map/ppermute | solution.py:23
  121.5 4.4 copy-start.11
  121.5 4.4 copy-start.12
  121.5 4.4 copy-start.13
  131.3 6.7 %collective-permute-start.6 = (bf16[1,128,256]{2,1,0:T(8,128)(2,1)S(1)}, bf16[1,128,256]{2,1,0:T(8,128)(2,1)S(1)}, u32[]{:S(2)}, u32[]{:S(2)}) collective-permute-start(bf16[1,128,256]{2,1,0:T(8,128)(2,1)S(1)} %get-tuple-element.19), channel_id=1, source_target_pairs={{0,8},{8,16},{16,24},{24,32},{32,40},{40,48},{48,56},{56,64},{64,7... | collective-permute-start | bytes 196616 | tf_op jit(solution)/shard_map/ppermute | solution.py:14
  135.9 8.0 %collective-permute-start.7 = (bf16[1,128,256]{2,1,0:T(8,128)(2,1)S(1)}, bf16[1,128,256]{2,1,0:T(8,128)(2,1)S(1)}, u32[]{:S(2)}, u32[]{:S(2)}) collective-permute-start(bf16[1,128,256]{2,1,0:T(8,128)(2,1)S(1)} %get-tuple-element.20), channel_id=1, source_target_pairs={{8,0},{16,8},{24,16},{32,24},{40,32},{48,40},{56,48},{64,56},{72,6... | collective-permute-start | bytes 196616 | tf_op jit(solution)/shard_map/ppermute | solution.py:15
  143.9 4.1 collective-permute-start.8
  146.4 4.7 %collective-permute-start.9 = (bf16[18,1,256]{2,1,0:T(2,128)(2,1)S(1)}, bf16[18,1,256]{2,1,0:T(2,128)(2,1)S(1)}, u32[]{:S(2)}, u32[]{:S(2)}) collective-permute-start(bf16[18,1,256]{2,1,0:T(2,128)(2,1)S(1)} %get-tuple-element.16), channel_id=1, source_target_pairs={{1,0},{2,1},{3,2},{4,3},{5,4},{6,5},{7,6},{9,8},{10,9},{11,10},{12... | collective-permute-start | bytes 27656 | tf_op jit(solution)/shard_map/ppermute | solution.py:15
  430.1 3.2 copy-start.1
  (9 other events, 13.8 us)
Sparse Core Ops, SparseCore 0:
  131.4 285.6 all-reduce.2
where the time goes:
time: 441 us; the launch traced here: 440 us
  waiting for transfers between devices  265 us (60%)
  local copies, waits for them, and re-layouts  74.5 us (17%)
  starting transfers between devices  31.7 us (7%)
  other arithmetic  28 us (6%)
  matrix products  24.6 us (6%)
  between operations  16.2 us (4%)
    psum x1, waiting for transfers between devices, on_device(): total_one, total_two = lax.psum((flat_one, flat_two), ('row', 'col'))  256 us
    slice x9, local copies, waits for them, and re-layouts, on_device(): act_pad[row_off:row_off + rows_here - 1:2, col_off:col_off + cols_here -...  19.8 us
    unnamed x62, local copies, waits for them, and re-layouts  18.9 us
    conv_general_dilated x12, local copies, waits for them, and re-layouts, conv_local(): lax.conv_general_dilated(source[None], kernel, (1, 1), padding, lhs_dilat...  15.6 us
    ppermute x4, starting transfers between devices, padded(): before = lax.ppermute(last, axis, up)  13 us
    dot_general x9, matrix products, on_device(): jnp.einsum('ijc,ije->ce', patch, cotangent, preferred_element_type=jnp.fl...  11.4 us
    ppermute x4, starting transfers between devices, passed_along(): return lax.ppermute(shard, axis, pairs)  11.4 us
    ppermute x4, waiting for transfers between devices, padded(): after = lax.ppermute(initial, axis, down)  9.07 us
  transfers between devices with their start and end apart: 13, of which 4 were waited for; matrix products, arithmetic and copies ran while one was open for 12% of the time, Pallas kernels for 0%

commit v1 on v0

--- a/solution.py
+++ b/solution.py
@@ -1,7 +1,17 @@
+import functools
 import jax
 import jax.numpy as jnp
 from jax import lax
 from jax.sharding import PartitionSpec as P
+
+
+def links_work(content, peer_axis, bus_axis):
+    for to_i in (peer_axis, bus_axis):
+        content = lax.psum(content, axis_name=to_i)
+    return content
+
+
+_store_ratios = functools.partial(links_work, peer_axis="row", bus_axis="col")
 
 
 def padded(shard, sides, width):
@@ -84,7 +94,7 @@
     )
     flat_one = grad_one.reshape(-1)
     flat_two = grad_two.reshape(-1)
-    total_one, total_two = lax.psum((flat_one, flat_two), ("row", "col"))
+    total_one, total_two = _store_ratios((flat_one, flat_two))
     update_one = (total_one * lax.rsqrt(jnp.mean(total_one * total_one) + 1e-06)).astype(
         jnp.bfloat16
     )

time: 441 us -> 459 us (1.041)
  waiting for transfers between devices: 265 us -> 284 us
    psum x1 -> x2, waiting for transfers between devices: 256 us -> 277 us  [links_work(): content = lax.psum(content, axis_name=to_i)]
  transfers between devices with their start and end apart: 13 -> 14, of which waited for: 4 -> 5; matrix products, arithmetic and copies ran while one was open for 12% -> 12% of each run, Pallas kernels for 0% -> 0%
where the time goes in v1:
time: 459 us; the launch traced here: 457 us
  waiting for transfers between devices  284 us (62%)
  local copies, waits for them, and re-layouts  74.5 us (16%)
  starting transfers between devices  29.8 us (6%)
  other arithmetic  28.1 us (6%)
  matrix products  24.6 us (5%)
  between operations  16.2 us (4%)
    psum x2, waiting for transfers between devices, links_work(): content = lax.psum(content, axis_name=to_i)  277 us
    slice x9, local copies, waits for them, and re-layouts, on_device(): act_pad[row_off:row_off + rows_here - 1:2, col_off:col_off + cols_here -...  19.8 us
    unnamed x62, local copies, waits for them, and re-layouts  19 us
    conv_general_dilated x12, local copies, waits for them, and re-layouts, conv_local(): lax.conv_general_dilated(source[None], kernel, (1, 1), padding, lhs_dilat...  15.6 us
    dot_general x9, matrix products, on_device(): jnp.einsum('ijc,ije->ce', patch, cotangent, preferred_element_type=jnp.fl...  11.4 us
    ppermute x4, starting transfers between devices, passed_along(): return lax.ppermute(shard, axis, pairs)  11.4 us
    ppermute x4, starting transfers between devices, padded(): before = lax.ppermute(last, axis, up)  10.5 us
  transfers between devices with their start and end apart: 14, of which 5 were waited for; matrix products, arithmetic and copies ran while one was open for 12% of the time, Pallas kernels for 0%

profile of v1, /device:TPU:2, one launch (start us, length us, event | category | flops | bytes accessed | tf_op | source)
XLA Modules:
  0.0 457.1 jit_solution(3779695067258547471)
XLA Ops:
  10.7 2.6 copy.37
  13.3 4.1 reshape.29
  22.8 3.4 collective-permute-start.2
  36.9 2.5 collective-permute-start.4
  48.0 4.4 maximum_bitcast_fusion
  52.3 3.9 copy.64
  56.2 2.4 pad.2.clone
  58.6 3.2 reshape.32
  63.9 3.0 convolution_select_fusion.1
  66.9 3.6 maximum_maximum_fusion
  74.8 2.7 slice.143
  77.5 2.7 slice.142
  80.1 2.7 slice.146
  82.9 2.7 slice.145
  91.1 4.4 collective-permute-start.10
  101.3 2.6 copy.65
  104.4 2.7 slice.141
  107.6 3.8 collective-permute-start.11
  115.7 2.7 slice.140
  118.5 2.7 slice.139
  127.9 3.4 copy.66
  131.4 204.3 %all-reduce.5.cloned.1.call-done = (f32[589824]{0:T(1024)}, f32[1179648]{0:T(1024)}) async-done(((f32[589824]{0:T(1024)}, f32[1179648]{0:T(1024)}), (f32[589824]{0:T(1024)}, f32[1179648]{0:T(1024)})) %all-reduce.5.cloned.1.call-update) | async-done | bytes 7077904 | tf_op jit(solution)/shard_map/psum | solution.py:10
  335.7 3.4 collective-permute-start.6
  339.1 2.5 collective-permute-start.7
  341.9 3.4 collective-permute-done.7
  348.2 3.2 collective-permute-done.9
  356.9 2.8 select_convert_fusion
  361.3 72.7 %all-reduce.7.cloned.1.call-done = (f32[589824]{0:T(1024)}, f32[1179648]{0:T(1024)}) async-done(((f32[589824]{0:T(1024)}, f32[1179648]{0:T(1024)}), (f32[589824]{0:T(1024)}, f32[1179648]{0:T(1024)})) %all-reduce.7.cloned.1.call-update) | async-done | bytes 7077904 | tf_op jit(solution)/shard_map/psum | solution.py:10
  434.0 3.6 multiply_reduce_fusion
  438.3 2.5 multiply_convert_fusion
  440.8 2.7 reshape.22
  443.5 2.9 multiply_reduce_fusion.1
  (143 shorter events, 70.7 us)
Async XLA Ops:
  7.2 328.5 %all-reduce.5.cloned.1.call-start = ((), (), s32[]{:S(2)}) async-start(), calls=%async_computation | async-start | bytes 14155776 | tf_op jit(solution)/shard_map/psum | solution.py:10
  17.4 4.6 %copy-start.9 = (bf16[16,128,256]{2,1,0:T(8,128)(2,1)S(1)}, bf16[16,128,256]{2,1,0:T(8,128)(2,1)}, u32[]{:S(2)}) copy-start(bf16[16,128,256]{2,1,0:T(8,128)(2,1)} %param.4) | copy-start | bytes 3145732
  20.8 9.8 %collective-permute-start = (f32[17,1,256]{2,1,0:T(1,128)S(1)}, f32[17,1,256]{2,1,0:T(1,128)S(1)}, u32[]{:S(2)}, u32[]{:S(2)}) collective-permute-start(f32[17,1,256]{2,1,0:T(1,128)S(1)} %slice.157), channel_id=1, source_target_pairs={{1,0},{2,1},{3,2},{4,3},{5,4},{6,5},{7,6},{9,8},{10,9},{11,10},{12... | collective-permute-start | bytes 52232 | tf_op jit(solution)/shard_map/ppermute | solution.py:33
  22.8 10.2 %collective-permute-start.2 = (bf16[1,128,256]{1,2,0:T(8,128)(2,1)S(1)}, bf16[1,128,256]{1,2,0:T(8,128)(2,1)S(1)}, u32[]{:S(2)}, u32[]{:S(2)}) collective-permute-start(bf16[1,128,256]{1,2,0:T(8,128)(2,1)S(1)} %get-tuple-element.23), channel_id=1, source_target_pairs={{0,8},{8,16},{16,24},{24,32},{32,40},{40,48},{48,56},{56,64},{64,7... | collective-permute-start | bytes 196616 | tf_op jit(solution)/shard_map/ppermute | solution.py:24
  26.2 6.8 %collective-permute-start.3 = (bf16[1,128,256]{1,2,0:T(8,128)(2,1)S(1)}, bf16[1,128,256]{1,2,0:T(8,128)(2,1)S(1)}, u32[]{:S(2)}, u32[]{:S(2)}) collective-permute-start(bf16[1,128,256]{1,2,0:T(8,128)(2,1)S(1)} %get-tuple-element.24), channel_id=1, source_target_pairs={{8,0},{16,8},{24,16},{32,24},{40,32},{48,40},{56,48},{64,56},{72,6... | collective-permute-start | bytes 196616 | tf_op jit(solution)/shard_map/ppermute | solution.py:25
  36.9 8.1 %collective-permute-start.4 = (bf16[18,1,256]{2,0,1:T(8,128)(2,1)S(1)}, bf16[18,1,256]{2,0,1:T(8,128)(2,1)S(1)}, u32[]{:S(2)}, u32[]{:S(2)}) collective-permute-start(bf16[18,1,256]{2,0,1:T(8,128)(2,1)S(1)} %copy.41), channel_id=1, source_target_pairs={{0,1},{1,2},{2,3},{3,4},{4,5},{5,6},{6,7},{8,9},{9,10},{10,11},{11... | collective-permute-start | bytes 27656 | tf_op jit(solution)/shard_map/ppermute | solution.py:24
  41.1 5.4 %collective-permute-start.5 = (bf16[18,1,256]{2,0,1:T(8,128)(2,1)S(1)}, bf16[18,1,256]{2,0,1:T(8,128)(2,1)S(1)}, u32[]{:S(2)}, u32[]{:S(2)}) collective-permute-start(bf16[18,1,256]{2,0,1:T(8,128)(2,1)S(1)} %copy.42), channel_id=1, source_target_pairs={{1,0},{2,1},{3,2},{4,3},{5,4},{6,5},{7,6},{9,8},{10,9},{11,10},{12... | collective-permute-start | bytes 27656 | tf_op jit(solution)/shard_map/ppermute | solution.py:25
  43.1 28.4 %collective-permute-start.1 = (bf16[1,128,256]{2,1,0:T(8,128)(2,1)}, bf16[1,128,256]{2,1,0:T(8,128)(2,1)S(1)}, u32[]{:S(2)}, u32[]{:S(2)}) collective-permute-start(bf16[1,128,256]{2,1,0:T(8,128)(2,1)} %fusion.41), channel_id=1, source_target_pairs={{8,0},{16,8},{24,16},{32,24},{40,32},{48,40},{56,48},{64,56},{72,6... | collective-permute-start | bytes 196616 | tf_op jit(solution)/shard_map/ppermute | solution.py:33
  63.8 3.0 copy-start.2
  63.8 3.0 copy-start.3
  85.6 2.0 copy-start.8
  85.6 2.7 copy-start.7
  90.1 5.5 %copy-start.14 = (bf16[8,64,512]{2,1,0:T(8,128)(2,1)S(1)}, bf16[8,64,512]{2,1,0:T(8,128)(2,1)}, u32[]{:S(2)}) copy-start(bf16[8,64,512]{2,1,0:T(8,128)(2,1)} %param.7) | copy-start | bytes 1572868
  90.1 5.5 %copy-start.21 = (bf16[8,64,256]{2,1,0:T(8,128)(2,1)S(1)}, bf16[8,64,256]{2,1,0:T(8,128)(2,1)}, u32[]{:S(2)}) copy-start(bf16[8,64,256]{2,1,0:T(8,128)(2,1)} %slice.143) | copy-start | bytes 786436
  90.5 6.1 %copy-start.20 = (bf16[8,64,256]{2,1,0:T(8,128)(2,1)S(1)}, bf16[8,64,256]{2,1,0:T(8,128)(2,1)}, u32[]{:S(2)}) copy-start(bf16[8,64,256]{2,1,0:T(8,128)(2,1)} %slice.142) | copy-start | bytes 786436
  91.1 6.7 %copy-start.19 = (bf16[8,64,256]{2,1,0:T(8,128)(2,1)S(1)}, bf16[8,64,256]{2,1,0:T(8,128)(2,1)}, u32[]{:S(2)}) copy-start(bf16[8,64,256]{2,1,0:T(8,128)(2,1)} %slice.146) | copy-start | bytes 786436
  91.1 7.8 %copy-start.18 = (bf16[8,64,256]{2,1,0:T(8,128)(2,1)S(1)}, bf16[8,64,256]{2,1,0:T(8,128)(2,1)}, u32[]{:S(2)}) copy-start(bf16[8,64,256]{2,1,0:T(8,128)(2,1)} %slice.145) | copy-start | bytes 786436
  91.1 12.8 %collective-permute-start.10 = (bf16[16,1,256]{2,1,0:T(2,128)(2,1)S(1)}, bf16[16,1,256]{2,1,0:T(2,128)(2,1)S(1)}, u32[]{:S(2)}, u32[]{:S(2)}) collective-permute-start(bf16[16,1,256]{2,1,0:T(2,128)(2,1)S(1)} %slice.178), channel_id=1, source_target_pairs={{0,1},{1,2},{2,3},{3,4},{4,5},{5,6},{6,7},{8,9},{9,10},{10,11},{11... | collective-permute-start | bytes 24584 | tf_op jit(solution)/shard_map/ppermute | solution.py:33
  103.9 9.7 %copy-start.22 = (bf16[16,1,256]{2,1,0:T(2,128)(2,1)}, bf16[16,1,256]{2,1,0:T(2,128)(2,1)S(1)}, u32[]{:S(2)}) copy-start(bf16[16,1,256]{2,1,0:T(2,128)(2,1)S(1)} %collective-permute-done.10) | copy-start | bytes 24580
  107.5 6.1 %copy-start.15 = (bf16[8,64,512]{2,1,0:T(8,128)(2,1)S(1)}, bf16[8,64,512]{2,1,0:T(8,128)(2,1)}, u32[]{:S(2)}) copy-start(bf16[8,64,512]{2,1,0:T(8,128)(2,1)} %param.7) | copy-start | bytes 1572868
  107.5 6.4 %copy-start.16 = (f32[1,256,512]{2,1,0:T(8,128)S(1)}, f32[1,256,512]{2,1,0:T(8,128)}, u32[]{:S(2)}) copy-start(f32[1,256,512]{2,1,0:T(8,128)} %convolution_bitcast_fusion) | copy-start | bytes 1572868
  107.6 6.4 %copy-start.17 = (f32[1,256,512]{2,1,0:T(8,128)S(1)}, f32[1,256,512]{2,1,0:T(8,128)}, u32[]{:S(2)}) copy-start(f32[1,256,512]{2,1,0:T(8,128)} %convolution_bitcast_fusion.1) | copy-start | bytes 1572868
  107.6 7.7 %collective-permute-start.11 = (bf16[1,129,256]{2,1,0:T(8,128)(2,1)S(1)}, bf16[1,129,256]{2,1,0:T(8,128)(2,1)S(1)}, u32[]{:S(2)}, u32[]{:S(2)}) collective-permute-start(bf16[1,129,256]{2,1,0:T(8,128)(2,1)S(1)} %fusion.42), channel_id=1, source_target_pairs={{0,8},{8,16},{16,24},{24,32},{32,40},{40,48},{48,56},{56,64},{64,7... | collective-permute-start | bytes 198152 | tf_op jit(solution)/shard_map/ppermute | solution.py:33
  121.6 4.4 copy-start.11
  121.6 4.4 copy-start.12
  121.6 4.4 copy-start.13
  131.3 302.7 %all-reduce.7.cloned.1.call-start = ((), (), s32[]{:S(2)}) async-start(), calls=%async_computation.1 | async-start | bytes 14155776 | tf_op jit(solution)/shard_map/psum | solution.py:10
  335.7 6.2 %collective-permute-start.6 = (bf16[1,128,256]{2,1,0:T(8,128)(2,1)S(1)}, bf16[1,128,256]{2,1,0:T(8,128)(2,1)S(1)}, u32[]{:S(2)}, u32[]{:S(2)}) collective-permute-start(bf16[1,128,256]{2,1,0:T(8,128)(2,1)S(1)} %get-tuple-element.21), channel_id=1, source_target_pairs={{0,8},{8,16},{16,24},{24,32},{32,40},{40,48},{48,56},{56,64},{64,7... | collective-permute-start | bytes 196616 | tf_op jit(solution)/shard_map/ppermute | solution.py:24
  339.1 6.2 %collective-permute-start.7 = (bf16[1,128,256]{2,1,0:T(8,128)(2,1)S(1)}, bf16[1,128,256]{2,1,0:T(8,128)(2,1)S(1)}, u32[]{:S(2)}, u32[]{:S(2)}) collective-permute-start(bf16[1,128,256]{2,1,0:T(8,128)(2,1)S(1)} %get-tuple-element.22), channel_id=1, source_target_pairs={{8,0},{16,8},{24,16},{32,24},{40,32},{48,40},{56,48},{64,56},{72,6... | collective-permute-start | bytes 196616 | tf_op jit(solution)/shard_map/ppermute | solution.py:25
  345.3 2.9 collective-permute-start.8
  346.6 4.8 %collective-permute-start.9 = (bf16[18,1,256]{2,1,0:T(2,128)(2,1)S(1)}, bf16[18,1,256]{2,1,0:T(2,128)(2,1)S(1)}, u32[]{:S(2)}, u32[]{:S(2)}) collective-permute-start(bf16[18,1,256]{2,1,0:T(2,128)(2,1)S(1)} %get-tuple-element.18), channel_id=1, source_target_pairs={{1,0},{2,1},{3,2},{4,3},{5,4},{6,5},{7,6},{9,8},{10,9},{11,10},{12... | collective-permute-start | bytes 27656 | tf_op jit(solution)/shard_map/ppermute | solution.py:25
  447.0 3.2 copy-start.1
  (10 other events, 15.7 us)
Sparse Core Ops, SparseCore 0:
  131.5 204.1 all-reduce.4
  338.2 95.7 all-reduce.6
